TPU v7x, 32 devices: a whole 2x2x4 slice. The times are simulated.
32 devices in a mesh: context: 4 (over z), head: 2 (over core), dp: 4 (over y, x).
Axes of the slice: x: 2, y: 2, z: 4, core: 2. Of those that a mesh axis runs over, the one named last changes fastest.
Arguments:
- lin_query: float32 [2048, 4096], P(('dp', 'context'), 'head'), parts along dimension 0, may hold values from -6 to 6
- lin_key: float32 [2048, 4096], P(('dp', 'context'), 'head'), parts along dimension 0, may hold values from -6 to 6
- lin_value: float32 [2048, 4096], P(('dp', 'context'), 'head'), parts along dimension 0, may hold values from -6 to 6
- lin_gate: float32 [2048, 4096], P(('dp', 'context'), 'head'), parts along dimension 0, may hold values from -8 to 8
- decay_rate: float32 [32, 2048], P('head', ('dp', 'context')), parts along dimension 1, may hold values from 0 to 1.5, as said below
- norm_gain: float32 [4096], P('head'), may hold values from 0.5 to 1.5
- sm_query: float32 [2048, 4096], P(('dp', 'context'), 'head'), parts along dimension 0, may hold values from -24 to 24
- sm_key: float32 [2048, 512], P(('dp', 'context'), 'head'), parts along dimension 0, may hold values from -24 to 24
- sm_value: float32 [2048, 512], P(('dp', 'context'), 'head'), parts along dimension 0, may hold values from -6 to 6
- doc_lengths: int32 [64], P('dp'), parts along dimension 0, may hold values from 1 to 384, 512 in all
Outputs:
- lin_out: float32 [2048, 4096], P(('dp', 'context'), 'head'), parts along dimension 0
- sm_out: float32 [2048, 4096], P(('dp', 'context'), 'head'), parts along dimension 0
There are 4 independent parts, one for each index of `dp`. A program takes and returns all parts, laid end to end along the dimension named above; an argument that names none is the same for every part. Nothing has to cross between parts.
Inputs may be any that keep to these rules, and one draw needn't show every extreme that they name: `doc_lengths`: the 16 lengths sum to 512 and the longest is exactly 384. `decay_rate`: positive rates.
All inputs are finite; a program needn't handle non-finite values.
Results may differ from a plain program's by a relative error of at most 0.0003.
Values sent between devices are 32-bit elements; how exact they have to be, the bound alone decides.
A program may use at most 192 MiB of HBM per device.

v0:
```python
import jax
import jax.numpy as jnp
from jax import lax
from jax.sharding import PartitionSpec as P

HEAD_DIM = 128
ROT_DIM = 64


rope_base = 10000000.0
norm_eps = 1e-05
highest = lax.Precision.HIGHEST


def entering(value, axis, join, neutral):
    count, mine = (lax.axis_size(axis), lax.axis_index(axis))
    pieces = jax.tree.map(lambda part: lax.all_gather(part, axis), value)
    subtotal = jax.tree.map(
        lambda part, zero: jnp.full_like(part, 0) + jnp.asarray(zero, part.dtype), value, neutral
    )

    def turn(position, subtotal):
        longer = join(subtotal, jax.tree.map(lambda part: part[position], pieces))
        return jax.tree.map(lambda new, old: jnp.where(position < mine, new, old), longer, subtotal)

    return lax.fori_loop(0, count - 1, turn, subtotal)


def doc_tables(doc_lengths):
    doc_ends = jnp.cumsum(doc_lengths)
    doc_starts = doc_ends - doc_lengths
    return (doc_starts, doc_ends)


def doc_number(tokens_at, doc_ends):
    return jnp.sum((doc_ends[None, :] <= tokens_at[:, None]).astype(jnp.int32), axis=1)


def doc_begin(tokens_at, doc_starts):
    picked = jnp.where(doc_starts[None, :] <= tokens_at[:, None], doc_starts[None, :], 0)
    return jnp.max(picked, axis=1)


def lightning_block(
    query_heads, key_heads, value_heads, forgetting_factors, first_token, doc_starts, doc_ends
):
    width = query_heads.shape[1]
    tokens_at = first_token + jnp.arange(width, dtype=jnp.int32)
    doc_ids = doc_number(tokens_at, doc_ends)
    begins = doc_begin(tokens_at, doc_starts)
    log_decay = jnp.cumsum(-forgetting_factors, axis=1)
    visible = (doc_ids[:, None] == doc_ids[None, :]) & (tokens_at[:, None] >= tokens_at[None, :])
    spread = jnp.where(visible[None], log_decay[:, :, None] - log_decay[:, None, :], 0.0)
    weight = jnp.where(visible[None], jnp.exp(spread), 0.0)
    scores = jnp.einsum("htd,hsd->hts", query_heads, key_heads, precision=highest) * weight
    intra = jnp.einsum("hts,hsd->htd", scores, value_heads, precision=highest)
    carried_rows = begins < first_token
    block_decay = jnp.where(carried_rows[-1], jnp.exp(log_decay[:, -1]), 0.0)
    in_tail = doc_ids == doc_ids[-1]
    tail_gap = jnp.where(in_tail[None], log_decay[:, -1:] - log_decay, 0.0)
    tail_weight = jnp.where(in_tail[None], jnp.exp(tail_gap), 0.0)
    block_inner = jnp.einsum(
        "htd,hte->hde", key_heads * tail_weight[:, :, None], value_heads, precision=highest
    )
    return (intra, log_decay, carried_rows, block_decay, block_inner)


def carried_term(query_heads, state, log_decay, carried_rows):
    reach_weight = jnp.where(carried_rows[None], jnp.exp(log_decay), 0.0)
    return (
        jnp.einsum("htd,hde->hte", query_heads, state, precision=highest) * reach_weight[:, :, None]
    )


def finish(attention, lin_gate, norm_gain):
    rows_count = attention.shape[0]
    per_head = attention.reshape(rows_count, -1, HEAD_DIM)
    mean_square = jnp.mean(per_head * per_head, axis=-1, keepdims=True)
    normed = (per_head / jnp.sqrt(mean_square + norm_eps)).reshape(rows_count, -1)
    return normed * norm_gain[None, :] * jax.nn.sigmoid(lin_gate)


def rotate(heads_in, positions):
    half = ROT_DIM // 2
    inverse = rope_base ** (-(2.0 * jnp.arange(half, dtype=jnp.float32)) / ROT_DIM)
    angle = positions.astype(jnp.float32)[:, None] * inverse[None, :]
    cosine = jnp.cos(angle)[:, None, :]
    sine = jnp.sin(angle)[:, None, :]
    first_half = heads_in[..., :half]
    second_half = heads_in[..., half:ROT_DIM]
    return jnp.concatenate(
        [
            first_half * cosine - second_half * sine,
            second_half * cosine + first_half * sine,
            heads_in[..., ROT_DIM:],
        ],
        axis=-1,
    )


def combine_states(earlier, later):
    return (earlier[0] * later[0], later[0][:, None, None] * earlier[1] + later[1])


def shards(
    lin_query,
    lin_key,
    lin_value,
    lin_gate,
    decay_rate,
    norm_gain,
    sm_query,
    sm_key,
    sm_value,
    doc_lengths,
):
    rows_here = lin_query.shape[0]
    lin_heads = lin_query.shape[1] // HEAD_DIM
    kv_local = sm_key.shape[1] // HEAD_DIM
    group = lin_heads // kv_local
    first_token = lax.axis_index("context") * rows_here
    doc_starts, doc_ends = doc_tables(doc_lengths)

    def split_heads(matrix):
        return matrix.reshape(rows_here, -1, HEAD_DIM).transpose(1, 0, 2)

    query_heads = split_heads(lin_query)
    intra, log_decay, carried_rows, block_decay, block_inner = lightning_block(
        query_heads,
        split_heads(lin_key),
        split_heads(lin_value),
        decay_rate,
        first_token,
        doc_starts,
        doc_ends,
    )
    identity = (jnp.ones_like(block_decay), jnp.zeros_like(block_inner))
    prior = entering((block_decay, block_inner), "context", combine_states, identity)
    state = prior[1]
    attention = intra + carried_term(query_heads, state, log_decay, carried_rows)
    attention = attention.transpose(1, 0, 2).reshape(rows_here, lin_heads * HEAD_DIM)
    lin_out = finish(attention, lin_gate, norm_gain)
    tokens_at = first_token + jnp.arange(rows_here, dtype=jnp.int32)
    positions = tokens_at - doc_begin(tokens_at, doc_starts)
    row_docs = doc_number(tokens_at, doc_ends)
    first_begin = doc_begin(first_token[None], doc_starts)[0]
    last_token = first_token + rows_here - 1
    queries = rotate(sm_query.reshape(rows_here, lin_heads, HEAD_DIM), positions)
    queries = queries.reshape(rows_here, kv_local, group, HEAD_DIM).transpose(1, 2, 0, 3)
    keys_rot = rotate(sm_key.reshape(rows_here, kv_local, HEAD_DIM), positions).reshape(
        rows_here, kv_local * HEAD_DIM
    )
    stacked = jnp.stack([keys_rot, sm_value])
    scale = HEAD_DIM ** (-0.5)
    start_carry = (
        jnp.full((kv_local, group, rows_here), -1e30, jnp.float32),
        jnp.zeros((kv_local, group, rows_here), jnp.float32),
        jnp.zeros((kv_local, group, rows_here, HEAD_DIM), jnp.float32),
    )
    piece = lax.all_gather(stacked, "context", axis=1, tiled=True)
    start = jnp.int32(0)
    count = piece.shape[1]
    relevant = (start <= last_token) & (start + count - 1 >= first_begin)

    def attend(current):
        top_old, total_old, summed_old = current
        key_index = jnp.arange(count, dtype=jnp.int32)
        key_docs = doc_number(key_index, doc_ends)
        visible = (
            (key_index[None, :] >= 0)
            & (key_docs[None, :] == row_docs[:, None])
            & (key_index[None, :] <= tokens_at[:, None])
        )
        key_rows = piece[0].reshape(count, kv_local, HEAD_DIM)
        value_rows = piece[1].reshape(count, kv_local, HEAD_DIM)
        scores = jnp.einsum("kgqd,nkd->kgqn", queries, key_rows, precision=highest) * scale
        masked = jnp.where(visible[None, None], scores, -jnp.inf)
        top_new = jnp.maximum(top_old, jnp.max(masked, axis=-1))
        weights = jnp.where(visible[None, None], jnp.exp(masked - top_new[..., None]), 0.0)
        total_new = jnp.sum(weights, axis=-1)
        summed_new = jnp.einsum("kgqn,nkd->kgqd", weights, value_rows, precision=highest)
        return (top_new, total_new, summed_new)

    def keep(current):
        return current

    final_carry = lax.cond(relevant, attend, keep, start_carry)
    mixed = final_carry[2] / final_carry[1][..., None]
    sm_out = mixed.transpose(2, 0, 1, 3).reshape(rows_here, lin_heads * HEAD_DIM)
    return (lin_out, sm_out)


def solution(mesh):
    in_specs = (
        P(("dp", "context"), "head"),
        P(("dp", "context"), "head"),
        P(("dp", "context"), "head"),
        P(("dp", "context"), "head"),
        P("head", ("dp", "context")),
        P("head"),
        P(("dp", "context"), "head"),
        P(("dp", "context"), "head"),
        P(("dp", "context"), "head"),
        P("dp"),
    )
    out_specs = (P(("dp", "context"), "head"), P(("dp", "context"), "head"))
    return jax.shard_map(shards, mesh=mesh, in_specs=in_specs, out_specs=out_specs, check_vma=False)
```

profile of v0, /device:TPU:0, one launch (start us, length us, event | category | flops | bytes accessed | tf_op | source)
XLA Modules:
  0.0 143.2 jit_solution(12342340220285167347)
XLA Ops:
  7.2 0.0 copy-start
  7.2 0.0 copy-start.3
  7.2 0.0 all-gather.5.cloned.1.call-start
  7.3 0.9 copy.87
  8.2 0.1 reduce.2
  8.3 1.3 fusion.22
  9.6 0.1 select_reduce_fusion.1
  9.7 1.0 copy.114
  10.7 1.0 copy.95
  11.7 0.1 multiply_cosine_fusion
  11.9 0.7 pad_maximum_fusion.1
  12.6 0.0 all-gather.5.cloned.1.call-update
  12.7 0.0 all-gather.7.cloned.1.call-start
  12.7 0.6 slice.38
  13.3 0.6 broadcast_compare_fusion
  14.0 0.6 slice.36
  14.5 0.7 neg.14
  15.2 1.6 %copy.111 = f32[128,2048]{0,1:T(8,128)S(1)} copy(f32[128,2048]{1,0:T(8,128)} %param.15) | data formatting | bytes 2097152 | tf_op jit(solution)/shard_map/reshape | solution.py:125
  16.8 0.3 reduce_window_sum.18
  17.1 0.9 slice_reduce_fusion
  18.0 0.1 select_bitcast_fusion
  18.0 2.2 %fusion.15 = f32[16,128,128]{2,1,0:T(8,128)} fusion(f32[16,128,128]{1,2,0:T(8,128)S(1)} %bitcast.95, f32[16,128]{1,0:T(8,128)S(1)} %get-tuple-element.166, f32[128,2048]{1,0:T(8,128)S(1)} %copy-done.3), kind=kOutput, calls=%fused_computation.29 | convolution fusion | flops 402915328 | bytes 3153920 | tf_op jit(solution)/shard_map/htd,hte->hde/dot_general | solution.py:62
  20.2 0.0 all-gather.7.cloned.1.call-update
  20.2 0.1 copy.97
  20.3 0.1 copy.99
  20.4 0.0 copy-done.1
  20.4 1.4 copy.121
  21.9 0.3 slice.52
  22.2 1.3 copy.117
  24.2 0.6 dynamic-slice
  25.4 0.2 dynamic-update-slice
  25.7 13.4 %all-reduce = f32[64]{0:T(128)S(1)} all-reduce(f32[64]{0:T(128)S(1)} %dynamic-update-slice), channel_id=2, replica_groups=mesh['context'=4,'head'=2,'dp'=4] {'context'}, use_global_device_ids=true, to_apply=%add | all-reduce | flops 64 | bytes 512
  39.1 0.1 reshape.343
  39.2 1.4 copy.120
  40.6 0.3 fusion.24
  41.0 0.0 copy-start.2
  41.0 0.6 multiply_subtract_fusion
  41.6 0.2 copy-done.4
  41.8 1.6 %pad_maximum_fusion = f32[128,16,128]{2,0,1:T(8,128)} fusion(f32[128,16,64]{2,0,1:T(8,128)S(1)} %copy-done.4, f32[128,16,32]{2,0,1:T(8,128)S(1)} %get-tuple-element.160, f32[128,16,32]{2,0,1:T(8,128)S(1)} %get-tuple-element.159), kind=kLoop, calls=%fused_computation.32 | loop fusion | flops 524288 | bytes 2097152 | tf_op jit(solution)/shard_map/concatenate | solution.py:91
  43.5 0.1 compare_and_fusion
  43.6 0.0 copy-done
  43.6 1.3 convolution_multiply_fusion
  44.9 2.0 %convolution_bitcast_fusion.1 = f32[128,16,128]{0,2,1:T(8,128)S(1)} fusion(f32[16,128,128]{2,1,0:T(8,128)S(1)} %convolution_multiply_fusion, f32[16,128,128]{2,0,1:T(8,128)S(1)} %bitcast.99), kind=kOutput, calls=%fused_computation.25 | convolution fusion | flops 402653184 | bytes 3145728 | tf_op jit(solution)/shard_map/hts,hsd->htd/dot_general | solution.py:56
  46.9 0.0 all-gather.5.cloned.1.call-done
  47.0 12.7 %conditional.1 = (f32[2,8,128]{2,1,0:T(8,128)S(1)}, f32[2,8,128,128]{3,2,1,0:T(8,128)S(1)}) conditional(s32[]{:T(128)} %convert_element_type.19, () %tuple.31, (s32[16]{0:T(128)S(1)}, s32[128]{0:T(128)S(1)}, s32[]{:T(128)}, s32[128]{0:T(128)S(1)}, f32[2,512,256]{1,2,0:T(8,128)}, /*index=5*/f32[2,8,128,128]{3,2,1,0:T(8,128)}) %tuple.68), branch_computations={%region_8.9_spmd, %region_9.13_spmd} | conditional | flops 3234027008 | bytes 18143316 | solution.py:187
  47.2 0.1 convert_reduce_fusion
  47.3 0.1 fusion.8
  47.4 1.3 fusion.23
  48.7 5.0 %fusion = (f32[2,8,128]{2,1,0:T(8,128)S(1)}, f32[2,8,128,512]{3,2,1,0:T(8,128)S(1)}) fusion(pred[128,512]{1,0:T(8,128)(4,1)S(1)} %fusion.8, f32[2,8,128,128]{3,2,1,0:T(8,128)} %get-tuple-element.111, f32[512,2,128,1]{0,2,3,1:T(8,128)S(1)} %bitcast.103), kind=kOutput, calls=%fused_computation.2 | convolution fusion | flops 1613756416 | bytes 5840896 | tf_op jit(solution)/shard_map/cond/branch_1_fun/kgqd,nkd->kgqn/dot_general | solution.py:176
  53.7 4.5 %fusion.1 = f32[2,8,128,128]{3,2,1,0:T(8,128)S(1)} fusion(f32[512,2,128,1]{0,2,3,1:T(8,128)S(1)} %bitcast.110, f32[2,8,128,512]{3,2,1,0:T(8,128)S(1)} %get-tuple-element.158, f32[2,8,128]{2,1,0:T(8,128)S(1)} %broadcast_maximum_fusion, pred[128,512]{1,0:T(8,128)(4,1)S(1)} %fusion.8), kind=kOutput, calls=%fused_computation.3 | convolution fusion | flops 1614807040 | bytes 5840896 | tf_op jit(solution)/shard_map/cond/branch_1_fun/kgqn,nkd->kgqd/dot_general | solution.py:181
  58.2 1.3 fusion.2
  59.7 0.3 divide_bitcast_fusion
  60.1 0.6 copy.101
  60.7 1.3 copy.144
  62.0 65.0 %all-gather.7.cloned.1.call-done = f32[64,128,128]{2,1,0:T(8,128)} async-done(((f32[16,128,128]{2,1,0:T(8,128)}), f32[64,128,128]{2,1,0:T(8,128)}) %all-gather.7.cloned.1.call-update) | async-done | bytes 4194320 | tf_op jit(solution)/shard_map/all_gather | solution.py:17
  127.0 4.5 %while.14 = (s32[]{:T(128)}, f32[16,128,128]{2,1,0:T(8,128)S(1)}, s32[]{:T(128)}, f32[4,16]{1,0:T(4,128)S(1)}, f32[4,16,128,128]{3,2,1,0:T(8,128)}, /*index=5*/s32[]{:T(128)}, s32[]{:T(128)}) while((s32[]{:T(128)}, f32[16,128,128]{2,1,0:T(8,128)S(1)}, s32[]{:T(128)}, f32[4,16]{1,0:T(4,128)S(1)}, f32[4,16,128,128]{3,2,1,0:T(8,128)}, ...), condition=%wide.region_5.6_spmd.clone, body=%wide.region_4.5_spmd.clone.sunk | while | flops 1048580 | bytes 3146025 | solution.py:26
  127.1 1.5 %fusion.35 = f32[16,128,128]{2,1,0:T(8,128)S(1)} fusion(f32[4,16,128,128]{3,2,1,0:T(8,128)} %get-tuple-element.222, s32[]{:T(128)} %get-tuple-element.211, f32[16,128,128]{2,1,0:T(8,128)S(1)} %get-tuple-element.212, f32[16]{0:T(128)S(1)} %dynamic-slice_bitcast_fusion.2, pred[]{:T(512)S(6)} %compare.3, pred[]{:T(512)S(6)} %lt.32), kind=kLoop, calls=%fused_computation.20.clone.1 | loop fusion | flops 1048576 | bytes 3145798 | tf_op jit(solution)/shard_map/while/body/eval_jaxpr/jit(_where)/select_n | solution.py:24
  128.5 1.5 %fusion.35 = f32[16,128,128]{2,1,0:T(8,128)S(1)} fusion(f32[4,16,128,128]{3,2,1,0:T(8,128)} %get-tuple-element.222, s32[]{:T(128)} %get-tuple-element.211, f32[16,128,128]{2,1,0:T(8,128)S(1)} %get-tuple-element.212, f32[16]{0:T(128)S(1)} %dynamic-slice_bitcast_fusion.2, pred[]{:T(512)S(6)} %compare.3, pred[]{:T(512)S(6)} %lt.32), kind=kLoop, calls=%fused_computation.20.clone.1 | loop fusion | flops 1048576 | bytes 3145798 | tf_op jit(solution)/shard_map/while/body/eval_jaxpr/jit(_where)/select_n | solution.py:24
  130.0 1.5 %fusion.35 = f32[16,128,128]{2,1,0:T(8,128)S(1)} fusion(f32[4,16,128,128]{3,2,1,0:T(8,128)} %get-tuple-element.222, s32[]{:T(128)} %get-tuple-element.211, f32[16,128,128]{2,1,0:T(8,128)S(1)} %get-tuple-element.212, f32[16]{0:T(128)S(1)} %dynamic-slice_bitcast_fusion.2, pred[]{:T(512)S(6)} %compare.3, pred[]{:T(512)S(6)} %lt.32), kind=kLoop, calls=%fused_computation.20.clone.1 | loop fusion | flops 1048576 | bytes 3145798 | tf_op jit(solution)/shard_map/while/body/eval_jaxpr/jit(_where)/select_n | solution.py:24
  131.5 0.0 copy-start.5
  131.5 1.9 %multiply_reduce_fusion = (f32[128,16]{0,1:T(8,128)S(1)}, f32[128,16,128]{0,2,1:T(8,128)S(1)}) fusion(f32[128,16,128]{0,2,1:T(8,128)S(1)} %convolution_bitcast_fusion.1, f32[128,16]{0,1:T(8,128)S(1)} %get-tuple-element.165, f32[16,128,128]{2,1,0:T(8,128)S(1)} %get-tuple-element.118, f32[128,2048]{1,0:T(8,128)S(1)} %copy-done), kind=kOutput, calls=%fused_computation.38 | convolution fusion | flops 403699712 | bytes 4210688 | tf_op jit(solution)/shard_map/htd,hde->hte/dot_general | solution.py:71
  133.4 0.1 broadcast_divide_fusion
  133.5 0.3 copy.91
  133.9 2.5 %divide_multiply_fusion = f32[128,2048]{1,0:T(8,128)} fusion(f32[128,2048]{1,0:T(8,128)} %param.17, f32[128,2048]{1,0:T(8,128)S(1)} %copy.91, f32[2048]{0:T(1024)S(1)} %copy-done.5), kind=kLoop, calls=%fused_computation.37 | loop fusion | flops 1310720 | bytes 3153920 | tf_op jit(solution)/shard_map/mul | solution.py:80
  (23 shorter events, 0.1 us)
Async XLA Ops:
  7.2 36.4 %copy-start = (f32[128,2048]{1,0:T(8,128)S(1)}, f32[128,2048]{1,0:T(8,128)}, u32[]{:S(2)}) copy-start(f32[128,2048]{1,0:T(8,128)} %param.14) | copy-start | bytes 3145732
  7.2 10.9 %copy-start.3 = (f32[128,2048]{1,0:T(8,128)S(1)}, f32[128,2048]{1,0:T(8,128)}, u32[]{:S(2)}) copy-start(f32[128,2048]{1,0:T(8,128)} %param.16) | copy-start | bytes 3145732
  7.2 39.8 %all-gather.5.cloned.1.call-start = ((), (), s32[]{:S(2)}) async-start(), calls=%async_computation | async-start | bytes 1310720 | tf_op jit(solution)/shard_map/all_gather | solution.py:160
  12.7 114.4 %all-gather.7.cloned.1.call-start = ((), (), s32[]{:S(2)}) async-start(), calls=%async_computation.1 | async-start | bytes 5242880 | tf_op jit(solution)/shard_map/all_gather | solution.py:17
  16.8 3.6 %copy-start.1 = (f32[128,2048]{0,1:T(8,128)}, f32[128,2048]{0,1:T(8,128)S(1)}, u32[]{:S(2)}) copy-start(f32[128,2048]{0,1:T(8,128)S(1)} %copy.111) | copy-start | bytes 3145732
  20.2 4.0 %copy-start.6 = (u32[32]{0:T(128)S(1)}, u32[32]{0:T(128)}, u32[]{:S(2)}) copy-start(u32[32]{0:T(128)} %constant.79) | copy-start | bytes 388
  40.6 1.2 copy-start.4
  41.0 2.6 %copy-start.2 = (f32[128,2048]{0,1:T(8,128)S(1)}, f32[128,2048]{0,1:T(8,128)}, u32[]{:S(2)}) copy-start(f32[128,2048]{0,1:T(8,128)} %copy-done.1) | copy-start | bytes 3145732
  131.5 2.4 %copy-start.5 = (f32[2048]{0:T(1024)S(1)}, f32[2048]{0:T(1024)}, u32[]{:S(2)}) copy-start(f32[2048]{0:T(1024)} %param.19) | copy-start | bytes 24580
Sparse Core Ops, SparseCore 0:
  12.8 32.9 all-gather.4
  47.9 79.0 all-gather.6
where the time goes:
time: 144 us; the launch traced here: 143 us
  waiting for transfers between devices  65.1 us (45%)
  matrix products  16.9 us (12%)
  other arithmetic  16.2 us (11%)
  between operations  15.6 us (11%)
  local copies, waits for them, and re-layouts  15.4 us (11%)
  blocking collectives  13.4 us (9%)
    all_gather x1, waiting for transfers between devices, entering(): pieces = jax.tree.map(lambda part: lax.all_gather(part, axis), value)  65 us
    unnamed x1, blocking collectives  13.4 us
    unnamed x22, local copies, waits for them, and re-layouts  7.58 us
    dot_general x1, matrix products, attend(): jnp.einsum('kgqd,nkd->kgqn', queries, key_rows, precision=highest) * scale  4.99 us
    dot_general x1, matrix products, attend(): jnp.einsum('kgqn,nkd->kgqd', weights, value_rows, precision=highest)  4.53 us
    select_n x3, other arithmetic, turn(): jnp.where(position < mine, new, old)  4.37 us
  transfers between devices with their start and end apart: 2, of which 1 were waited for; matrix products, arithmetic and copies ran while one was open for 24% of the time, Pallas kernels for 0%

commit v1 on v0

v1 whole, which is shorter than its diff:
```python
import functools

import jax
import jax.numpy as jnp
import numpy as np
from jax import lax
from jax.experimental import pallas as pl
from jax.experimental.pallas import tpu as pltpu
from jax.sharding import PartitionSpec as P

HEAD = 128
ROT = 64
BASE = 10000000.0
EPS = 1e-05
MESH = pl.DeviceIdType.MESH
HIGHEST = lax.Precision.HIGHEST
F32 = jnp.float32
BF16 = jnp.bfloat16
PAIR = 2


def rotary_tables(n, rows):
    half = ROT // 2
    exponent = -(2.0 * np.arange(half, dtype=np.float32)) / np.float32(ROT)
    inverse = np.power(np.float32(BASE), exponent.astype(np.float32)).astype(np.float64)
    place = np.arange(rows)[None, :] - rows * np.arange(n)[:, None]
    angle = place.reshape(-1, 1) * inverse[None, :]
    cosine = np.ones((n * rows, HEAD), np.float32)
    sine = np.zeros((n * rows, HEAD), np.float32)
    cosine[:, :half] = cosine[:, half:ROT] = np.cos(angle)
    sine[:, :half] = -np.sin(angle)
    sine[:, half:ROT] = np.sin(angle)
    return np.stack([cosine, sine])


def dot(a, b, contract, precision=None):
    return lax.dot_general(
        a, b, ((contract[0], contract[1]), ((), ())), precision=precision, preferred_element_type=F32
    )


def split(x):
    high = x.astype(BF16)
    return high, (x - high.astype(F32)).astype(BF16)


def rotated(x, cosine, sine):
    half = ROT // 2
    lane = lax.broadcasted_iota(jnp.int32, x.shape, 1)
    swapped = jnp.where(lane < half, pltpu.roll(x, HEAD - half, 1), pltpu.roll(x, half, 1))
    return x * cosine + swapped * sine


def kernel(
    n, rows, heads, kv, docs,
    len_ref, rate_ref, gain_ref, sk_hbm, sv_hbm, lk_hbm, lv_hbm, lq_hbm, sq_hbm, gate_hbm, tab_hbm,
    lin_hbm, sm_hbm,
    kvbuf, lk, lv, lq, sq, gate, tab, lin, sm, logd, begin, bias, keys, vals, inner, entered,
    load_sem, kv_send, kv_recv, st_send, st_recv, lin_sem, sm_sem,
):
    me = lax.axis_index("context")
    first = me * rows
    pairs = heads // PAIR
    group = heads // kv
    right = {"context": me + 1}

    loads = []
    for place, (src, dst) in enumerate(
        [
            (lk_hbm, lk), (lv_hbm, lv), (lq_hbm, lq), (sk_hbm, kvbuf.at[0, 0]), (sv_hbm, kvbuf.at[0, 1]),
            (tab_hbm, tab), (sq_hbm, sq), (gate_hbm, gate),
        ]
    ):
        copy = pltpu.make_async_copy(src, dst, load_sem.at[place])
        copy.start()
        loads.append(copy)

    def kv_copy(slot, which):
        src = (sk_hbm, sv_hbm)[which] if slot == 0 else kvbuf.at[slot, which]
        return pltpu.make_async_remote_copy(
            src_ref=src, dst_ref=kvbuf.at[slot + 1, which],
            send_sem=kv_send.at[slot, which], recv_sem=kv_recv.at[slot + 1, which],
            device_id=right, device_id_type=MESH,
        )

    def kv_arrival(slot, which):
        return pltpu.make_async_remote_copy(
            src_ref=kvbuf.at[slot, which], dst_ref=kvbuf.at[slot, which],
            send_sem=kv_send.at[slot, which], recv_sem=kv_recv.at[slot, which],
            device_id=right, device_id_type=MESH,
        )

    def state_copy(pair):
        here = pl.ds(pair * PAIR, PAIR)
        return pltpu.make_async_remote_copy(
            src_ref=inner.at[here], dst_ref=entered.at[here],
            send_sem=st_send.at[pair], recv_sem=st_recv.at[pair],
            device_id=right, device_id_type=MESH,
        )

    barrier = pltpu.get_barrier_semaphore()

    @pl.when(me > 0)
    def _():
        pl.semaphore_signal(barrier, inc=1, device_id={"context": me - 1}, device_id_type=MESH)

    @pl.when(me < n - 1)
    def _():
        pl.semaphore_wait(barrier, 1)
        kv_copy(0, 0).start()
        kv_copy(0, 1).start()

    row = first + lax.broadcasted_iota(jnp.int32, (rows, rows), 0)
    lane = lax.broadcasted_iota(jnp.int32, (rows, rows), 1)
    last = first + rows - 1
    start = jnp.int32(0)
    starts = jnp.zeros((rows, rows), jnp.int32)
    start_last = jnp.int32(0)
    for d in range(docs):
        starts = jnp.where(row >= start, start, starts)
        start_last = jnp.where(last >= start, start, start_last)
        start = start + len_ref[d]
    begin[...] = starts
    for slot in range(n):
        column = rows * (me - slot) + lane
        bias[:, slot * rows:(slot + 1) * rows] = jnp.where(
            (column >= starts) & (column <= row), 0.0, -jnp.inf
        ).astype(F32)
    upper = jnp.where(
        lax.broadcasted_iota(jnp.int32, (rows, rows), 0) <= lane, 1.0, 0.0
    ).astype(F32)
    logd[...] = dot(-rate_ref[...], upper, ((1,), (0,)), HIGHEST)

    def lanes(head):
        return pl.ds(pl.multiple_of(head * HEAD, HEAD), HEAD)

    def log_rows(head):
        one = logd[pl.ds(head, 1), :]
        return (
            jnp.broadcast_to(one, (rows, rows)),
            jnp.broadcast_to(one[:, rows - 1:], (rows, rows)),
        )

    loads[0].wait()
    loads[1].wait()
    in_tail = first + lane >= start_last

    def inner_pair(pair, _):
        for j in range(PAIR):
            head = pair * PAIR + j
            along, end = log_rows(head)
            weight = jnp.exp(jnp.where(in_tail, end - along, -jnp.inf))
            turned = lk[:, lanes(head)].T * weight
            inner[head] = dot(turned, lv[:, lanes(head)], ((1,), (0,)), HIGHEST)

        @pl.when(me == 0)
        def _():
            if n > 1:
                state_copy(pair).start()

        return 0

    lax.fori_loop(0, pairs, inner_pair, 0)

    def place_keys(slot):
        at = slice(slot * rows, (slot + 1) * rows)
        cosine, sine = tab[0, at, :], tab[1, at, :]
        for g in range(kv):
            features = slice(g * HEAD, (g + 1) * HEAD)
            high, low = split(rotated(kvbuf[slot, 0, :, features], cosine, sine))
            keys[g, at, :] = jnp.concatenate([high, high], axis=1)
            keys[g, n * rows + slot * rows:n * rows + (slot + 1) * rows, :] = jnp.concatenate(
                [low, low], axis=1
            )
            high, low = split(kvbuf[slot, 1, :, features])
            both = jnp.concatenate([high, low], axis=1)
            vals[g, at, :] = both
            vals[g, n * rows + slot * rows:n * rows + (slot + 1) * rows, :] = both

    def receive(slot):
        @pl.when(me >= slot)
        def _():
            for which in range(2):
                kv_arrival(slot, which).wait_recv()
                if slot < n - 1:
                    @pl.when(me < n - 1)
                    def _():
                        kv_copy(slot, which).start()
            place_keys(slot)

        @pl.when(me < slot)
        def _():
            for g in range(kv):
                for base in (0, n * rows):
                    at = slice(base + slot * rows, base + (slot + 1) * rows)
                    keys[g, at, :] = jnp.zeros((rows, 2 * HEAD), BF16)
                    vals[g, at, :] = jnp.zeros((rows, 2 * HEAD), BF16)

    loads[2].wait()
    for copy in loads[3:6]:
        copy.wait()
    if n > 1:
        receive(1)
    place_keys(0)

    def intra_pair(pair, _):
        visible = bias[:, 0:rows] == 0.0
        carried = begin[...] < first
        for j in range(PAIR):
            head = pair * PAIR + j
            along, _end = log_rows(head)
            down = along.T
            weight = jnp.exp(jnp.where(visible, down - along, -jnp.inf))
            query = lq[:, lanes(head)]
            scores = dot(query, lk[:, lanes(head)], ((1,), (1,)), HIGHEST) * weight
            lin[:, lanes(head)] = dot(scores, lv[:, lanes(head)], ((1,), (0,)), HIGHEST)
            reach = jnp.exp(jnp.where(carried, down, -jnp.inf))
            lq[:, lanes(head)] = query * reach
        return 0

    lax.fori_loop(0, pairs, intra_pair, 0)
    for slot in range(2, n):
        receive(slot)

    loads[6].wait()
    loads[7].wait()

    @pl.when(me == 0)
    def _():
        entered[...] = jnp.zeros_like(entered)

    scale = HEAD ** -0.5

    def finish_pair(pair, _):
        @pl.when(me > 0)
        def _():
            state_copy(pair).wait_recv()

        for j in range(PAIR):
            head = pair * PAIR + j
            _along, end = log_rows(head)
            decay = jnp.exp(jnp.where(start_last < first, end, -jnp.inf))
            inner_out = decay * entered[head]

            @pl.when(me > 0)
            def _():
                inner[head] = inner[head] + inner_out

        @pl.when((me > 0) & (me < n - 1))
        def _():
            state_copy(pair).start()

        queries = []
        for j in range(PAIR):
            head = pair * PAIR + j
            attention = lin[:, lanes(head)] + dot(
                lq[:, lanes(head)], entered[head], ((1,), (0,)), HIGHEST
            )
            square = jnp.mean(attention * attention, axis=1, keepdims=True)
            normed = attention * lax.rsqrt(square + EPS) * gain_ref[:, lanes(head)]
            lin[:, lanes(head)] = normed / (1.0 + jnp.exp(-gate[:, lanes(head)]))
            turned = rotated(sq[:, lanes(head)], tab[0, 0:rows, :], tab[1, 0:rows, :]) * scale
            queries.append(jnp.concatenate(split(turned), axis=1))
        query = jnp.concatenate(queries, axis=0)
        g = lax.div(pair * PAIR, group)
        width = n * rows
        products = dot(query, keys[g], ((1,), (1,)))
        scores = products[:, :width] + products[:, width:]
        scores = scores + jnp.concatenate([bias[...]] * PAIR, axis=0)
        weights = jnp.exp(scores - jnp.max(scores, axis=1, keepdims=True))
        total = jnp.sum(weights, axis=1, keepdims=True)
        mixed = dot(jnp.concatenate(split(weights), axis=1), vals[g], ((1,), (0,)))
        mixed = (mixed[:, :HEAD] + mixed[:, HEAD:]) / total
        for j in range(PAIR):
            sm[:, lanes(pair * PAIR + j)] = mixed[j * rows:(j + 1) * rows]
        out_copy(lin, lin_hbm, lin_sem, pair).start()
        out_copy(sm, sm_hbm, sm_sem, pair).start()
        return 0

    def out_copy(src, dst, sem, pair):
        at = pl.ds(pl.multiple_of(pair * PAIR * HEAD, PAIR * HEAD), PAIR * HEAD)
        return pltpu.make_async_copy(src.at[:, at], dst.at[:, at], sem.at[pair])

    lax.fori_loop(0, pairs, finish_pair, 0)

    def drain(pair, _):
        out_copy(lin, lin_hbm, lin_sem, pair).wait()
        out_copy(sm, sm_hbm, sm_sem, pair).wait()

        @pl.when(me < n - 1)
        def _():
            state_copy(pair).wait_send()

        return 0

    lax.fori_loop(0, pairs, drain, 0)
    for slot in range(n - 1):
        @pl.when((me < n - 1) & (me >= slot))
        def _():
            kv_copy(slot, 0).wait_send()
            kv_copy(slot, 1).wait_send()


def shards(
    n, lin_query, lin_key, lin_value, lin_gate, decay_rate, norm_gain, sm_query, sm_key, sm_value, doc_lengths
):
    rows, features = lin_query.shape
    heads, kv = features // HEAD, sm_key.shape[1] // HEAD
    docs = doc_lengths.shape[0]
    pairs = heads // PAIR
    width = n * rows
    vmem = pl.BlockSpec(memory_space=pltpu.VMEM)
    anywhere = pl.BlockSpec(memory_space=pl.ANY)
    big = pltpu.VMEM((rows, features), F32)
    table = jnp.asarray(rotary_tables(n, rows))
    out = jax.ShapeDtypeStruct((rows, features), F32)
    call = pl.pallas_call(
        functools.partial(kernel, n, rows, heads, kv, docs),
        out_shape=(out, out),
        in_specs=[pl.BlockSpec(memory_space=pltpu.SMEM), vmem, vmem] + [anywhere] * 8,
        out_specs=(anywhere, anywhere),
        scratch_shapes=[
            pltpu.VMEM((n, 2, rows, kv * HEAD), F32),
            big, big, big, big, big,
            pltpu.VMEM((2, width, HEAD), F32),
            big, big,
            pltpu.VMEM((heads, rows), F32),
            pltpu.VMEM((rows, rows), jnp.int32),
            pltpu.VMEM((rows, width), F32),
            pltpu.VMEM((kv, 2 * width, 2 * HEAD), BF16),
            pltpu.VMEM((kv, 2 * width, 2 * HEAD), BF16),
            pltpu.VMEM((heads, HEAD, HEAD), F32),
            pltpu.VMEM((heads, HEAD, HEAD), F32),
            pltpu.SemaphoreType.DMA((8,)),
            pltpu.SemaphoreType.DMA((n, 2)),
            pltpu.SemaphoreType.DMA((n, 2)),
            pltpu.SemaphoreType.DMA((pairs,)),
            pltpu.SemaphoreType.DMA((pairs,)),
            pltpu.SemaphoreType.DMA((pairs,)),
            pltpu.SemaphoreType.DMA((pairs,)),
        ],
        compiler_params=pltpu.CompilerParams(
            collective_id=0, has_side_effects=True, vmem_limit_bytes=60 * 1024 * 1024
        ),
    )
    return call(
        doc_lengths, decay_rate, norm_gain.reshape(1, features), sm_key, sm_value,
        lin_key, lin_value, lin_query, sm_query, lin_gate, table,
    )


def solution(mesh):
    tokens = P(("dp", "context"), "head")
    in_specs = (
        tokens, tokens, tokens, tokens, P("head", ("dp", "context")), P("head"),
        tokens, tokens, tokens, P("dp"),
    )
    return jax.shard_map(
        functools.partial(shards, mesh.shape["context"]),
        mesh=mesh, in_specs=in_specs, out_specs=(tokens, tokens), check_vma=False,
    )
```

time: 144 us -> 52.1 us (0.36)
  the two profiles are of different devices: /device:TPU:0 before, /device:TPU:24 now
where the time goes in v1:
time: 52.1 us; the launch traced here: 51.9 us
  Pallas kernels  47.9 us (92%)
  local copies, waits for them, and re-layouts  3.36 us (6%)
  between operations  0.65 us (1%)
    pallas_call x1, Pallas kernels, shards(): call(doc_lengths, decay_rate, norm_gain.reshape(1, features), sm_key, sm_...  47.9 us
    unnamed x4, local copies, waits for them, and re-layouts  3.36 us

profile of v1, /device:TPU:24, one launch (start us, length us, event | category | flops | bytes accessed | tf_op | source)
XLA Modules:
  0.0 51.9 jit_solution(5718190100549671766)
XLA Ops:
  0.6 47.9 %shard_map.122 = (f32[128,2048]{1,0:T(8,128)}, f32[128,2048]{1,0:T(8,128)}) custom-call(s32[16]{0:T(128)} %len_ref.1, f32[16,128]{1,0:T(8,128)} %rate_ref.1, f32[1,2048]{1,0:T(1,128)} %bitcast.1, f32[128,256]{1,0:T(8,128)} %sk_hbm.1, f32[128,256]{1,0:T(8,128)} %sv_hbm.1, f32[128,2048]{1,0:T(8,128)} %lk_hbm.1, f32[128,2048]{1,0:T(8,128)} %lv_hbm.1, ...), custom_call_target="tpu_custom_call" | custom-call | tf_op jit(solution)/shard_map/pallas_call | solution.py:346
  48.5 0.0 copy-start
  48.6 2.4 %copy.15 = f32[128,2048]{1,0:T(8,128)} copy(f32[128,2048]{1,0:T(8,128)} %get-tuple-element.4) | data formatting | bytes 2097152
  50.9 0.0 copy-done
  50.9 1.0 %copy.16 = f32[128,2048]{1,0:T(8,128)} copy(f32[128,2048]{1,0:T(8,128)S(1)} %copy-done) | data formatting | bytes 2097152
Async XLA Ops:
  48.5 2.4 %copy-start = (f32[128,2048]{1,0:T(8,128)S(1)}, f32[128,2048]{1,0:T(8,128)}, u32[]{:S(2)}) copy-start(f32[128,2048]{1,0:T(8,128)} %get-tuple-element.5) | copy-start | bytes 3145732

commit v2 on v1

--- a/solution.py
+++ b/solution.py
@@ -44,6 +44,24 @@
     return high, (x - high.astype(F32)).astype(BF16)
 
 
+def halves(x):
+    return jnp.concatenate(split(x), axis=1)
+
+
+def against_rows(lhs, rhs):
+    high, low = split(rhs)
+    wide = jnp.concatenate(
+        [jnp.concatenate([high, high], axis=1), jnp.concatenate([low, low], axis=1)], axis=0
+    )
+    out = dot(lhs, wide, ((1,), (1,)))
+    return out[:, :HEAD] + out[:, HEAD:]
+
+
+def against_columns(lhs, rhs):
+    out = dot(lhs, jnp.concatenate([rhs, rhs], axis=0), ((1,), (0,)))
+    return out[:, :HEAD] + out[:, HEAD:]
+
+
 def rotated(x, cosine, sine):
     half = ROT // 2
     lane = lax.broadcasted_iota(jnp.int32, x.shape, 1)
@@ -55,7 +73,7 @@
     n, rows, heads, kv, docs,
     len_ref, rate_ref, gain_ref, sk_hbm, sv_hbm, lk_hbm, lv_hbm, lq_hbm, sq_hbm, gate_hbm, tab_hbm,
     lin_hbm, sm_hbm,
-    kvbuf, lk, lv, lq, sq, gate, tab, lin, sm, logd, begin, bias, keys, vals, inner, entered,
+    kvbuf, lk, lv, lq, sq, gate, tab, lin, sm, logd, begin, bias, keys, vals, lvh, lqh, inner, entered,
     load_sem, kv_send, kv_recv, st_send, st_recv, lin_sem, sm_sem,
 ):
     me = lax.axis_index("context")
@@ -151,7 +169,9 @@
             along, end = log_rows(head)
             weight = jnp.exp(jnp.where(in_tail, end - along, -jnp.inf))
             turned = lk[:, lanes(head)].T * weight
-            inner[head] = dot(turned, lv[:, lanes(head)], ((1,), (0,)), HIGHEST)
+            both = halves(lv[:, lanes(head)])
+            lvh[head] = both
+            inner[head] = against_columns(halves(turned), both)
 
         @pl.when(me == 0)
         def _():
@@ -212,10 +232,10 @@
             down = along.T
             weight = jnp.exp(jnp.where(visible, down - along, -jnp.inf))
             query = lq[:, lanes(head)]
-            scores = dot(query, lk[:, lanes(head)], ((1,), (1,)), HIGHEST) * weight
-            lin[:, lanes(head)] = dot(scores, lv[:, lanes(head)], ((1,), (0,)), HIGHEST)
+            scores = against_rows(halves(query), lk[:, lanes(head)]) * weight
+            lin[:, lanes(head)] = against_columns(halves(scores), lvh[head])
             reach = jnp.exp(jnp.where(carried, down, -jnp.inf))
-            lq[:, lanes(head)] = query * reach
+            lqh[head] = halves(query * reach)
         return 0
 
     lax.fori_loop(0, pairs, intra_pair, 0)
@@ -253,9 +273,7 @@
         queries = []
         for j in range(PAIR):
             head = pair * PAIR + j
-            attention = lin[:, lanes(head)] + dot(
-                lq[:, lanes(head)], entered[head], ((1,), (0,)), HIGHEST
-            )
+            attention = lin[:, lanes(head)] + against_columns(lqh[head], halves(entered[head]))
             square = jnp.mean(attention * attention, axis=1, keepdims=True)
             normed = attention * lax.rsqrt(square + EPS) * gain_ref[:, lanes(head)]
             lin[:, lanes(head)] = normed / (1.0 + jnp.exp(-gate[:, lanes(head)]))
@@ -329,6 +347,8 @@
             pltpu.VMEM((rows, width), F32),
             pltpu.VMEM((kv, 2 * width, 2 * HEAD), BF16),
             pltpu.VMEM((kv, 2 * width, 2 * HEAD), BF16),
+            pltpu.VMEM((heads, rows, 2 * HEAD), BF16),
+            pltpu.VMEM((heads, rows, 2 * HEAD), BF16),
             pltpu.VMEM((heads, HEAD, HEAD), F32),
             pltpu.VMEM((heads, HEAD, HEAD), F32),
             pltpu.SemaphoreType.DMA((8,)),

time: 52.1 us -> 49.3 us (0.946)
  Pallas kernels: 47.9 us -> 45.1 us
    pallas_call x1, Pallas kernels: 47.9 us -> 45.1 us  [shards(): call(doc_lengths, decay_rate, norm_gain.reshape(1, features), sm_key, sm_...]
where the time goes in v2:
time: 49.3 us; the launch traced here: 49.1 us
  Pallas kernels  45.1 us (91%)
  local copies, waits for them, and re-layouts  3.36 us (7%)
  between operations  0.65 us (1%)
    pallas_call x1, Pallas kernels, shards(): call(doc_lengths, decay_rate, norm_gain.reshape(1, features), sm_key, sm_...  45.1 us
    unnamed x4, local copies, waits for them, and re-layouts  3.36 us

profile of v2, /device:TPU:24, one launch (start us, length us, event | category | flops | bytes accessed | tf_op | source)
XLA Modules:
  0.0 49.1 jit_solution(13047692544249495437)
XLA Ops:
  0.6 45.1 %shard_map.122 = (f32[128,2048]{1,0:T(8,128)}, f32[128,2048]{1,0:T(8,128)}) custom-call(s32[16]{0:T(128)} %len_ref.1, f32[16,128]{1,0:T(8,128)} %rate_ref.1, f32[1,2048]{1,0:T(1,128)} %bitcast.1, f32[128,256]{1,0:T(8,128)} %sk_hbm.1, f32[128,256]{1,0:T(8,128)} %sv_hbm.1, f32[128,2048]{1,0:T(8,128)} %lk_hbm.1, f32[128,2048]{1,0:T(8,128)} %lv_hbm.1, ...), custom_call_target="tpu_custom_call" | custom-call | tf_op jit(solution)/shard_map/pallas_call | solution.py:366
  45.7 0.0 copy-start
  45.7 2.4 %copy.15 = f32[128,2048]{1,0:T(8,128)} copy(f32[128,2048]{1,0:T(8,128)} %get-tuple-element.4) | data formatting | bytes 2097152
  48.1 0.0 copy-done
  48.1 1.0 %copy.16 = f32[128,2048]{1,0:T(8,128)} copy(f32[128,2048]{1,0:T(8,128)S(1)} %copy-done) | data formatting | bytes 2097152
Async XLA Ops:
  45.7 2.4 %copy-start = (f32[128,2048]{1,0:T(8,128)S(1)}, f32[128,2048]{1,0:T(8,128)}, u32[]{:S(2)}) copy-start(f32[128,2048]{1,0:T(8,128)} %get-tuple-element.5) | copy-start | bytes 3145732

commit v3 on v2

--- a/solution.py
+++ b/solution.py
@@ -17,6 +17,7 @@
 F32 = jnp.float32
 BF16 = jnp.bfloat16
 PAIR = 2
+PARTS = 4
 
 
 def rotary_tables(n, rows):
@@ -71,9 +72,9 @@
 
 def kernel(
     n, rows, heads, kv, docs,
-    len_ref, rate_ref, gain_ref, sk_hbm, sv_hbm, lk_hbm, lv_hbm, lq_hbm, sq_hbm, gate_hbm, tab_hbm,
+    len_ref, rate_hbm, gain_hbm, sk_hbm, sv_hbm, lk_hbm, lv_hbm, lq_hbm, sq_hbm, gate_hbm, tab_hbm,
     lin_hbm, sm_hbm,
-    kvbuf, lk, lv, lq, sq, gate, tab, lin, sm, logd, begin, bias, keys, vals, lvh, lqh, inner, entered,
+    rate_ref, gain_ref, kvbuf, lk, lv, lq, sq, gate, tab, lin, sm, logd, begin, bias, keys, vals, lvh, lqh, inner, entered,
     load_sem, kv_send, kv_recv, st_send, st_recv, lin_sem, sm_sem,
 ):
     me = lax.axis_index("context")
@@ -82,16 +83,24 @@
     group = heads // kv
     right = {"context": me + 1}
 
-    loads = []
-    for place, (src, dst) in enumerate(
-        [
-            (lk_hbm, lk), (lv_hbm, lv), (lq_hbm, lq), (sk_hbm, kvbuf.at[0, 0]), (sv_hbm, kvbuf.at[0, 1]),
-            (tab_hbm, tab), (sq_hbm, sq), (gate_hbm, gate),
-        ]
-    ):
-        copy = pltpu.make_async_copy(src, dst, load_sem.at[place])
+    barrier = pltpu.get_barrier_semaphore()
+
+    @pl.when(me > 0)
+    def _():
+        pl.semaphore_signal(barrier, inc=1, device_id={"context": me - 1}, device_id_type=MESH)
+
+    loads = [
+        pltpu.make_async_copy(src, dst, load_sem.at[place])
+        for place, (src, dst) in enumerate(
+            [
+                (rate_hbm, rate_ref), (lk_hbm, lk), (lv_hbm, lv), (sk_hbm, kvbuf.at[0, 0]),
+                (sv_hbm, kvbuf.at[0, 1]), (tab_hbm, tab), (lq_hbm, lq), (sq_hbm, sq), (gate_hbm, gate),
+                (gain_hbm, gain_ref),
+            ]
+        )
+    ]
+    for copy in loads[:3]:
         copy.start()
-        loads.append(copy)
 
     def kv_copy(slot, which):
         src = (sk_hbm, sv_hbm)[which] if slot == 0 else kvbuf.at[slot, which]
@@ -116,17 +125,14 @@
             device_id=right, device_id_type=MESH,
         )
 
-    barrier = pltpu.get_barrier_semaphore()
-
-    @pl.when(me > 0)
-    def _():
-        pl.semaphore_signal(barrier, inc=1, device_id={"context": me - 1}, device_id_type=MESH)
-
     @pl.when(me < n - 1)
     def _():
         pl.semaphore_wait(barrier, 1)
         kv_copy(0, 0).start()
         kv_copy(0, 1).start()
+
+    for copy in loads[3:]:
+        copy.start()
 
     row = first + lax.broadcasted_iota(jnp.int32, (rows, rows), 0)
     lane = lax.broadcasted_iota(jnp.int32, (rows, rows), 1)
@@ -147,6 +153,7 @@
     upper = jnp.where(
         lax.broadcasted_iota(jnp.int32, (rows, rows), 0) <= lane, 1.0, 0.0
     ).astype(F32)
+    loads[0].wait()
     logd[...] = dot(-rate_ref[...], upper, ((1,), (0,)), HIGHEST)
 
     def lanes(head):
@@ -159,8 +166,8 @@
             jnp.broadcast_to(one[:, rows - 1:], (rows, rows)),
         )
 
-    loads[0].wait()
     loads[1].wait()
+    loads[2].wait()
     in_tail = first + lane >= start_last
 
     def inner_pair(pair, _):
@@ -216,16 +223,36 @@
                     keys[g, at, :] = jnp.zeros((rows, 2 * HEAD), BF16)
                     vals[g, at, :] = jnp.zeros((rows, 2 * HEAD), BF16)
 
-    loads[2].wait()
     for copy in loads[3:6]:
         copy.wait()
     if n > 1:
         receive(1)
     place_keys(0)
-
-    def intra_pair(pair, _):
+    for slot in range(2, n):
+        receive(slot)
+    for copy in loads[6:]:
+        copy.wait()
+
+    @pl.when(me == 0)
+    def _():
+        entered[...] = jnp.zeros_like(entered)
+
+    scale = HEAD ** -0.5
+
+    def finish_pair(pair, _):
+        @pl.when((me > 0) & (me < n - 1))
+        def _():
+            state_copy(pair).wait_recv()
+            for j in range(PAIR):
+                head = pair * PAIR + j
+                _along, end = log_rows(head)
+                decay = jnp.exp(jnp.where(start_last < first, end, -jnp.inf))
+                inner[head] = inner[head] + decay * entered[head]
+            state_copy(pair).start()
+
         visible = bias[:, 0:rows] == 0.0
         carried = begin[...] < first
+        queries = []
         for j in range(PAIR):
             head = pair * PAIR + j
             along, _end = log_rows(head)
@@ -235,50 +262,9 @@
             scores = against_rows(halves(query), lk[:, lanes(head)]) * weight
             lin[:, lanes(head)] = against_columns(halves(scores), lvh[head])
             reach = jnp.exp(jnp.where(carried, down, -jnp.inf))
-            lqh[head] = halves(query * reach)
-        return 0
-
-    lax.fori_loop(0, pairs, intra_pair, 0)
-    for slot in range(2, n):
-        receive(slot)
-
-    loads[6].wait()
-    loads[7].wait()
-
-    @pl.when(me == 0)
-    def _():
-        entered[...] = jnp.zeros_like(entered)
-
-    scale = HEAD ** -0.5
-
-    def finish_pair(pair, _):
-        @pl.when(me > 0)
-        def _():
-            state_copy(pair).wait_recv()
-
-        for j in range(PAIR):
-            head = pair * PAIR + j
-            _along, end = log_rows(head)
-            decay = jnp.exp(jnp.where(start_last < first, end, -jnp.inf))
-            inner_out = decay * entered[head]
-
-            @pl.when(me > 0)
-            def _():
-                inner[head] = inner[head] + inner_out
-
-        @pl.when((me > 0) & (me < n - 1))
-        def _():
-            state_copy(pair).start()
-
-        queries = []
-        for j in range(PAIR):
-            head = pair * PAIR + j
-            attention = lin[:, lanes(head)] + against_columns(lqh[head], halves(entered[head]))
-            square = jnp.mean(attention * attention, axis=1, keepdims=True)
-            normed = attention * lax.rsqrt(square + EPS) * gain_ref[:, lanes(head)]
-            lin[:, lanes(head)] = normed / (1.0 + jnp.exp(-gate[:, lanes(head)]))
+            lqh[j] = halves(query * reach)
             turned = rotated(sq[:, lanes(head)], tab[0, 0:rows, :], tab[1, 0:rows, :]) * scale
-            queries.append(jnp.concatenate(split(turned), axis=1))
+            queries.append(halves(turned))
         query = jnp.concatenate(queries, axis=0)
         g = lax.div(pair * PAIR, group)
         width = n * rows
@@ -287,12 +273,24 @@
         scores = scores + jnp.concatenate([bias[...]] * PAIR, axis=0)
         weights = jnp.exp(scores - jnp.max(scores, axis=1, keepdims=True))
         total = jnp.sum(weights, axis=1, keepdims=True)
-        mixed = dot(jnp.concatenate(split(weights), axis=1), vals[g], ((1,), (0,)))
+        mixed = dot(halves(weights), vals[g], ((1,), (0,)))
         mixed = (mixed[:, :HEAD] + mixed[:, HEAD:]) / total
         for j in range(PAIR):
             sm[:, lanes(pair * PAIR + j)] = mixed[j * rows:(j + 1) * rows]
+        out_copy(sm, sm_hbm, sm_sem, pair).start()
+
+        if n > 1:
+            @pl.when(me == n - 1)
+            def _():
+                state_copy(pair).wait_recv()
+
+        for j in range(PAIR):
+            head = pair * PAIR + j
+            attention = lin[:, lanes(head)] + against_columns(lqh[j], halves(entered[head]))
+            square = jnp.mean(attention * attention, axis=1, keepdims=True)
+            normed = attention * lax.rsqrt(square + EPS) * gain_ref[:, lanes(head)]
+            lin[:, lanes(head)] = normed / (1.0 + jnp.exp(-gate[:, lanes(head)]))
         out_copy(lin, lin_hbm, lin_sem, pair).start()
-        out_copy(sm, sm_hbm, sm_sem, pair).start()
         return 0
 
     def out_copy(src, dst, sem, pair):
@@ -317,6 +315,18 @@
         def _():
             kv_copy(slot, 0).wait_send()
             kv_copy(slot, 1).wait_send()
+
+
+def hand_over(rows, lin_in, sm_in, lin_out, sm_out, sem):
+    copies = []
+    for which, (src, dst) in enumerate([(lin_in, lin_out), (sm_in, sm_out)]):
+        for part in range(PARTS):
+            at = pl.ds(part * (rows // PARTS), rows // PARTS)
+            copies.append(pltpu.make_async_copy(src.at[at], dst.at[at], sem.at[which, part]))
+    for copy in copies:
+        copy.start()
+    for copy in copies:
+        copy.wait()
 
 
 def shards(
@@ -327,7 +337,6 @@
     docs = doc_lengths.shape[0]
     pairs = heads // PAIR
     width = n * rows
-    vmem = pl.BlockSpec(memory_space=pltpu.VMEM)
     anywhere = pl.BlockSpec(memory_space=pl.ANY)
     big = pltpu.VMEM((rows, features), F32)
     table = jnp.asarray(rotary_tables(n, rows))
@@ -335,9 +344,11 @@
     call = pl.pallas_call(
         functools.partial(kernel, n, rows, heads, kv, docs),
         out_shape=(out, out),
-        in_specs=[pl.BlockSpec(memory_space=pltpu.SMEM), vmem, vmem] + [anywhere] * 8,
+        in_specs=[pl.BlockSpec(memory_space=pltpu.SMEM)] + [anywhere] * 10,
         out_specs=(anywhere, anywhere),
         scratch_shapes=[
+            pltpu.VMEM((heads, rows), F32),
+            pltpu.VMEM((1, features), F32),
             pltpu.VMEM((n, 2, rows, kv * HEAD), F32),
             big, big, big, big, big,
             pltpu.VMEM((2, width, HEAD), F32),
@@ -348,10 +359,10 @@
             pltpu.VMEM((kv, 2 * width, 2 * HEAD), BF16),
             pltpu.VMEM((kv, 2 * width, 2 * HEAD), BF16),
             pltpu.VMEM((heads, rows, 2 * HEAD), BF16),
-            pltpu.VMEM((heads, rows, 2 * HEAD), BF16),
+            pltpu.VMEM((PAIR, rows, 2 * HEAD), BF16),
             pltpu.VMEM((heads, HEAD, HEAD), F32),
             pltpu.VMEM((heads, HEAD, HEAD), F32),
-            pltpu.SemaphoreType.DMA((8,)),
+            pltpu.SemaphoreType.DMA((10,)),
             pltpu.SemaphoreType.DMA((n, 2)),
             pltpu.SemaphoreType.DMA((n, 2)),
             pltpu.SemaphoreType.DMA((pairs,)),
@@ -363,10 +374,18 @@
             collective_id=0, has_side_effects=True, vmem_limit_bytes=60 * 1024 * 1024
         ),
     )
-    return call(
+    results = call(
         doc_lengths, decay_rate, norm_gain.reshape(1, features), sm_key, sm_value,
         lin_key, lin_value, lin_query, sm_query, lin_gate, table,
     )
+    return pl.pallas_call(
+        functools.partial(hand_over, rows),
+        out_shape=(out, out),
+        in_specs=[anywhere] * 2,
+        out_specs=(anywhere, anywhere),
+        scratch_shapes=[pltpu.SemaphoreType.DMA((2, PARTS))],
+        compiler_params=pltpu.CompilerParams(vmem_limit_bytes=60 * 1024 * 1024),
+    )(*results)
 
 
 def solution(mesh):

time: 49.3 us -> 110 us (2.23)
  Pallas kernels: 45.1 us -> 109 us
  local copies, waits for them, and re-layouts: 3.36 us -> 0 us
    pallas_call x0 -> x1, Pallas kernels: none -> 64.7 us  [shards(): pl.pallas_call(functools.partial(hand_over, rows), out_shape=(out, out),...]
    unnamed x4 -> x0, local copies, waits for them, and re-layouts: 3.36 us -> none
where the time goes in v3:
time: 110 us
  Pallas kernels  109 us (99%)
    pallas_call x1, Pallas kernels, shards(): pl.pallas_call(functools.partial(hand_over, rows), out_shape=(out, out),...  64.7 us
    pallas_call x1, Pallas kernels, shards(): call(doc_lengths, decay_rate, norm_gain.reshape(1, features), sm_key, sm_...  44.2 us

profile of v3, /device:TPU:24, one launch (start us, length us, event | category | flops | bytes accessed | tf_op | source)
XLA Modules:
  0.0 109.6 jit_solution(11175504264167694645)
XLA Ops:
  0.6 44.2 %shard_map.122 = (f32[128,2048]{1,0:T(8,128)}, f32[128,2048]{1,0:T(8,128)}) custom-call(s32[16]{0:T(128)} %len_ref.1, f32[16,128]{1,0:T(8,128)} %rate_hbm.1, f32[1,2048]{1,0:T(1,128)} %bitcast.1, f32[128,256]{1,0:T(8,128)} %sk_hbm.1, f32[128,256]{1,0:T(8,128)} %sv_hbm.1, f32[128,2048]{1,0:T(8,128)} %lk_hbm.1, f32[128,2048]{1,0:T(8,128)} %lv_hbm.1, ...), custom_call_target="tpu_custom_call" | custom-call | tf_op jit(solution)/shard_map/pallas_call | solution.py:377
  44.9 64.7 %shard_map.123 = (f32[128,2048]{1,0:T(8,128)}, f32[128,2048]{1,0:T(8,128)}) custom-call(f32[128,2048]{1,0:T(8,128)} %get-tuple-element.4.lin_in, f32[128,2048]{1,0:T(8,128)} %get-tuple-element.5.sm_in), custom_call_target="tpu_custom_call" | custom-call | tf_op jit(solution)/shard_map/pallas_call | solution.py:381

commit v4 on v3

--- a/solution.py
+++ b/solution.py
@@ -317,15 +317,20 @@
             kv_copy(slot, 1).wait_send()
 
 
-def hand_over(rows, lin_in, sm_in, lin_out, sm_out, sem):
-    copies = []
-    for which, (src, dst) in enumerate([(lin_in, lin_out), (sm_in, sm_out)]):
-        for part in range(PARTS):
-            at = pl.ds(part * (rows // PARTS), rows // PARTS)
-            copies.append(pltpu.make_async_copy(src.at[at], dst.at[at], sem.at[which, part]))
-    for copy in copies:
+def hand_over(rows, lin_in, sm_in, lin_out, sm_out, held, in_sem, out_sem):
+    arrive, leave = [], []
+    for part in range(PARTS):
+        at = pl.ds(part * (rows // PARTS), rows // PARTS)
+        for which, (src, dst) in enumerate([(lin_in, lin_out), (sm_in, sm_out)]):
+            slot = held.at[which, at]
+            arrive.append(pltpu.make_async_copy(src.at[at], slot, in_sem.at[which, part]))
+            leave.append(pltpu.make_async_copy(slot, dst.at[at], out_sem.at[which, part]))
+    for copy in arrive:
         copy.start()
-    for copy in copies:
+    for come, go in zip(arrive, leave):
+        come.wait()
+        go.start()
+    for copy in leave:
         copy.wait()
 
 
@@ -383,7 +388,11 @@
         out_shape=(out, out),
         in_specs=[anywhere] * 2,
         out_specs=(anywhere, anywhere),
-        scratch_shapes=[pltpu.SemaphoreType.DMA((2, PARTS))],
+        scratch_shapes=[
+            pltpu.VMEM((2, rows, features), F32),
+            pltpu.SemaphoreType.DMA((2, PARTS)),
+            pltpu.SemaphoreType.DMA((2, PARTS)),
+        ],
         compiler_params=pltpu.CompilerParams(vmem_limit_bytes=60 * 1024 * 1024),
     )(*results)
 

time: 110 us -> 47.4 us (0.43)
  Pallas kernels: 109 us -> 46.6 us
    pallas_call x1, Pallas kernels: 64.7 us -> 2.39 us  [shards(): pl.pallas_call(functools.partial(hand_over, rows), out_shape=(out, out),...]
where the time goes in v4:
time: 47.4 us; the launch traced here: 47.3 us
  Pallas kernels  46.6 us (98%)
  between operations  0.64 us (1%)
    pallas_call x1, Pallas kernels, shards(): call(doc_lengths, decay_rate, norm_gain.reshape(1, features), sm_key, sm_...  44.2 us
    pallas_call x1, Pallas kernels, shards(): pl.pallas_call(functools.partial(hand_over, rows), out_shape=(out, out),...  2.39 us

profile of v4, /device:TPU:24, one launch (start us, length us, event | category | flops | bytes accessed | tf_op | source)
XLA Modules:
  0.0 47.3 jit_solution(17717126171524947937)
XLA Ops:
  0.6 44.2 %shard_map.122 = (f32[128,2048]{1,0:T(8,128)}, f32[128,2048]{1,0:T(8,128)}) custom-call(s32[16]{0:T(128)} %len_ref.1, f32[16,128]{1,0:T(8,128)} %rate_hbm.1, f32[1,2048]{1,0:T(1,128)} %bitcast.1, f32[128,256]{1,0:T(8,128)} %sk_hbm.1, f32[128,256]{1,0:T(8,128)} %sv_hbm.1, f32[128,2048]{1,0:T(8,128)} %lk_hbm.1, f32[128,2048]{1,0:T(8,128)} %lv_hbm.1, ...), custom_call_target="tpu_custom_call" | custom-call | tf_op jit(solution)/shard_map/pallas_call | solution.py:382
  44.9 2.4 %shard_map.123 = (f32[128,2048]{1,0:T(8,128)}, f32[128,2048]{1,0:T(8,128)}) custom-call(f32[128,2048]{1,0:T(8,128)} %get-tuple-element.4.lin_in, f32[128,2048]{1,0:T(8,128)} %get-tuple-element.5.sm_in), custom_call_target="tpu_custom_call" | custom-call | tf_op jit(solution)/shard_map/pallas_call | solution.py:386

commit v5 on v4

--- a/solution.py
+++ b/solution.py
@@ -74,20 +74,27 @@
     n, rows, heads, kv, docs,
     len_ref, rate_hbm, gain_hbm, sk_hbm, sv_hbm, lk_hbm, lv_hbm, lq_hbm, sq_hbm, gate_hbm, tab_hbm,
     lin_hbm, sm_hbm,
-    rate_ref, gain_ref, kvbuf, lk, lv, lq, sq, gate, tab, lin, sm, logd, begin, bias, keys, vals, lvh, lqh, inner, entered,
-    load_sem, kv_send, kv_recv, st_send, st_recv, lin_sem, sm_sem,
+    rate_ref, gain_ref, kvbuf, lk, lv, lq, sq, gate, tab, lin, sm, logd, begin, bias, keys, vals, lvh, lqh, reached, asked, inner, entered,
+    load_sem, kv_send, kv_recv, st_send, st_recv, lin_sem, sm_sem, ask_send, ask_recv,
 ):
     me = lax.axis_index("context")
     first = me * rows
     pairs = heads // PAIR
     group = heads // kv
     right = {"context": me + 1}
+    pack = n > 1 and 4 * (n - 1) == 3 * n
+    packed_pairs = -(-2 * kv // PAIR) if pack else 0
 
     barrier = pltpu.get_barrier_semaphore()
 
     @pl.when(me > 0)
     def _():
         pl.semaphore_signal(barrier, inc=1, device_id={"context": me - 1}, device_id_type=MESH)
+
+    if pack:
+        @pl.when(me == n - 2)
+        def _():
+            pl.semaphore_signal(barrier, inc=1, device_id=right, device_id_type=MESH)
 
     loads = [
         pltpu.make_async_copy(src, dst, load_sem.at[place])
@@ -125,12 +132,27 @@
             device_id=right, device_id_type=MESH,
         )
 
+    def query_copy(pair):
+        at = pl.ds(pl.multiple_of(pair * PAIR * HEAD, PAIR * HEAD), PAIR * HEAD)
+        return pltpu.make_async_remote_copy(
+            src_ref=lq_hbm.at[:, at], dst_ref=asked.at[:, at],
+            send_sem=ask_send.at[pair], recv_sem=ask_recv.at[pair],
+            device_id={"context": me - 1}, device_id_type=MESH,
+        )
+
     @pl.when(me < n - 1)
     def _():
         pl.semaphore_wait(barrier, 1)
         kv_copy(0, 0).start()
         kv_copy(0, 1).start()
 
+    if pack:
+        @pl.when(me == n - 1)
+        def _():
+            pl.semaphore_wait(barrier, 1)
+            for pair in range(pairs):
+                query_copy(pair).start()
+
     for copy in loads[3:]:
         copy.start()
 
@@ -139,10 +161,11 @@
     last = first + rows - 1
     start = jnp.int32(0)
     starts = jnp.zeros((rows, rows), jnp.int32)
-    start_last = jnp.int32(0)
+    start_last = start_next = jnp.int32(0)
     for d in range(docs):
         starts = jnp.where(row >= start, start, starts)
         start_last = jnp.where(last >= start, start, start_last)
+        start_next = jnp.where(last + 1 >= start, start, start_next)
         start = start + len_ref[d]
     begin[...] = starts
     for slot in range(n):
@@ -189,31 +212,38 @@
 
     lax.fori_loop(0, pairs, inner_pair, 0)
 
-    def place_keys(slot):
+    def place_keys(slot, source):
         at = slice(slot * rows, (slot + 1) * rows)
         cosine, sine = tab[0, at, :], tab[1, at, :]
         for g in range(kv):
-            features = slice(g * HEAD, (g + 1) * HEAD)
-            high, low = split(rotated(kvbuf[slot, 0, :, features], cosine, sine))
+            high, low = split(rotated(source(0, g), cosine, sine))
             keys[g, at, :] = jnp.concatenate([high, high], axis=1)
             keys[g, n * rows + slot * rows:n * rows + (slot + 1) * rows, :] = jnp.concatenate(
                 [low, low], axis=1
             )
-            high, low = split(kvbuf[slot, 1, :, features])
+            high, low = split(source(1, g))
             both = jnp.concatenate([high, low], axis=1)
             vals[g, at, :] = both
             vals[g, n * rows + slot * rows:n * rows + (slot + 1) * rows, :] = both
 
+    def from_slot(slot):
+        return lambda which, g: kvbuf[slot, which, :, g * HEAD:(g + 1) * HEAD]
+
     def receive(slot):
         @pl.when(me >= slot)
         def _():
+            if pack and slot == n - 1:
+                for pair in range(packed_pairs):
+                    state_copy(pair).wait_recv()
+                place_keys(slot, lambda which, g: entered[which * kv + g])
+                return
             for which in range(2):
                 kv_arrival(slot, which).wait_recv()
-                if slot < n - 1:
+                if slot < n - 1 - pack:
                     @pl.when(me < n - 1)
                     def _():
                         kv_copy(slot, which).start()
-            place_keys(slot)
+            place_keys(slot, from_slot(slot))
 
         @pl.when(me < slot)
         def _():
@@ -227,7 +257,7 @@
         copy.wait()
     if n > 1:
         receive(1)
-    place_keys(0)
+    place_keys(0, from_slot(0))
     for slot in range(2, n):
         receive(slot)
     for copy in loads[6:]:
@@ -238,6 +268,18 @@
         entered[...] = jnp.zeros_like(entered)
 
     scale = HEAD ** -0.5
+
+    def answer(pair):
+        query_copy(pair).wait_recv()
+        kept = row - (n - 2) * rows >= start_next
+        for j in range(PAIR):
+            head = pair * PAIR + j
+            inner[head] = against_columns(halves(asked[:, lanes(head)]), halves(inner[head]))
+
+            @pl.when(head < 2 * kv)
+            def _():
+                piece = kvbuf[n - 2, lax.div(head, kv), :, lanes(lax.rem(head, kv))]
+                inner[head] = jnp.where(kept, piece, inner[head])
 
     def finish_pair(pair, _):
         @pl.when((me > 0) & (me < n - 1))
@@ -248,6 +290,10 @@
                 _along, end = log_rows(head)
                 decay = jnp.exp(jnp.where(start_last < first, end, -jnp.inf))
                 inner[head] = inner[head] + decay * entered[head]
+            if pack:
+                @pl.when(me == n - 2)
+                def _():
+                    answer(pair)
             state_copy(pair).start()
 
         visible = bias[:, 0:rows] == 0.0
@@ -263,6 +309,7 @@
             lin[:, lanes(head)] = against_columns(halves(scores), lvh[head])
             reach = jnp.exp(jnp.where(carried, down, -jnp.inf))
             lqh[j] = halves(query * reach)
+            reached[j] = reach
             turned = rotated(sq[:, lanes(head)], tab[0, 0:rows, :], tab[1, 0:rows, :]) * scale
             queries.append(halves(turned))
         query = jnp.concatenate(queries, axis=0)
@@ -280,13 +327,24 @@
         out_copy(sm, sm_hbm, sm_sem, pair).start()
 
         if n > 1:
-            @pl.when(me == n - 1)
+            @pl.when((me == n - 1) & (pair >= packed_pairs))
             def _():
                 state_copy(pair).wait_recv()
 
         for j in range(PAIR):
             head = pair * PAIR + j
-            attention = lin[:, lanes(head)] + against_columns(lqh[j], halves(entered[head]))
+            if pack:
+                @pl.when(me == n - 1)
+                def _():
+                    lin[:, lanes(head)] += reached[j] * entered[head]
+
+                @pl.when(me < n - 1)
+                def _():
+                    lin[:, lanes(head)] += against_columns(lqh[j], halves(entered[head]))
+
+                attention = lin[:, lanes(head)]
+            else:
+                attention = lin[:, lanes(head)] + against_columns(lqh[j], halves(entered[head]))
             square = jnp.mean(attention * attention, axis=1, keepdims=True)
             normed = attention * lax.rsqrt(square + EPS) * gain_ref[:, lanes(head)]
             lin[:, lanes(head)] = normed / (1.0 + jnp.exp(-gate[:, lanes(head)]))
@@ -307,10 +365,15 @@
         def _():
             state_copy(pair).wait_send()
 
+        if pack:
+            @pl.when(me == n - 1)
+            def _():
+                query_copy(pair).wait_send()
+
         return 0
 
     lax.fori_loop(0, pairs, drain, 0)
-    for slot in range(n - 1):
+    for slot in range(n - 1 - pack):
         @pl.when((me < n - 1) & (me >= slot))
         def _():
             kv_copy(slot, 0).wait_send()
@@ -365,11 +428,15 @@
             pltpu.VMEM((kv, 2 * width, 2 * HEAD), BF16),
             pltpu.VMEM((heads, rows, 2 * HEAD), BF16),
             pltpu.VMEM((PAIR, rows, 2 * HEAD), BF16),
+            pltpu.VMEM((PAIR, rows, rows), F32),
+            big,
             pltpu.VMEM((heads, HEAD, HEAD), F32),
             pltpu.VMEM((heads, HEAD, HEAD), F32),
             pltpu.SemaphoreType.DMA((10,)),
             pltpu.SemaphoreType.DMA((n, 2)),
             pltpu.SemaphoreType.DMA((n, 2)),
+            pltpu.SemaphoreType.DMA((pairs,)),
+            pltpu.SemaphoreType.DMA((pairs,)),
             pltpu.SemaphoreType.DMA((pairs,)),
             pltpu.SemaphoreType.DMA((pairs,)),
             pltpu.SemaphoreType.DMA((pairs,)),

time: 47.4 us -> 46.8 us (0.987)
  Pallas kernels: 46.6 us -> 46.1 us
    pallas_call x1, Pallas kernels: 44.2 us -> 43.7 us  [shards(): call(doc_lengths, decay_rate, norm_gain.reshape(1, features), sm_key, sm_...]
where the time goes in v5:
time: 46.8 us; the launch traced here: 46.7 us
  Pallas kernels  46.1 us (99%)
  between operations  0.64 us (1%)
    pallas_call x1, Pallas kernels, shards(): call(doc_lengths, decay_rate, norm_gain.reshape(1, features), sm_key, sm_...  43.7 us
    pallas_call x1, Pallas kernels, shards(): pl.pallas_call(functools.partial(hand_over, rows), out_shape=(out, out),...  2.39 us

profile of v5, /device:TPU:24, one launch (start us, length us, event | category | flops | bytes accessed | tf_op | source)
XLA Modules:
  0.0 46.7 jit_solution(754310759379729969)
XLA Ops:
  0.6 43.7 %shard_map.122 = (f32[128,2048]{1,0:T(8,128)}, f32[128,2048]{1,0:T(8,128)}) custom-call(s32[16]{0:T(128)} %len_ref.1, f32[16,128]{1,0:T(8,128)} %rate_hbm.1, f32[1,2048]{1,0:T(1,128)} %bitcast.1, f32[128,256]{1,0:T(8,128)} %sk_hbm.1, f32[128,256]{1,0:T(8,128)} %sv_hbm.1, f32[128,2048]{1,0:T(8,128)} %lk_hbm.1, f32[128,2048]{1,0:T(8,128)} %lv_hbm.1, ...), custom_call_target="tpu_custom_call" | custom-call | tf_op jit(solution)/shard_map/pallas_call | solution.py:449
  44.3 2.4 %shard_map.123 = (f32[128,2048]{1,0:T(8,128)}, f32[128,2048]{1,0:T(8,128)}) custom-call(f32[128,2048]{1,0:T(8,128)} %get-tuple-element.4.lin_in, f32[128,2048]{1,0:T(8,128)} %get-tuple-element.5.sm_in), custom_call_target="tpu_custom_call" | custom-call | tf_op jit(solution)/shard_map/pallas_call | solution.py:453

commit v6 on v5

--- a/solution.py
+++ b/solution.py
@@ -124,11 +124,10 @@
             device_id=right, device_id_type=MESH,
         )
 
-    def state_copy(pair):
-        here = pl.ds(pair * PAIR, PAIR)
+    def state_copy(head):
         return pltpu.make_async_remote_copy(
-            src_ref=inner.at[here], dst_ref=entered.at[here],
-            send_sem=st_send.at[pair], recv_sem=st_recv.at[pair],
+            src_ref=inner.at[head], dst_ref=entered.at[head],
+            send_sem=st_send.at[head], recv_sem=st_recv.at[head],
             device_id=right, device_id_type=MESH,
         )
 
@@ -206,7 +205,8 @@
         @pl.when(me == 0)
         def _():
             if n > 1:
-                state_copy(pair).start()
+                for j in range(PAIR):
+                    state_copy(pair * PAIR + j).start()
 
         return 0
 
@@ -233,8 +233,8 @@
         @pl.when(me >= slot)
         def _():
             if pack and slot == n - 1:
-                for pair in range(packed_pairs):
-                    state_copy(pair).wait_recv()
+                for head in range(packed_pairs * PAIR):
+                    state_copy(head).wait_recv()
                 place_keys(slot, lambda which, g: entered[which * kv + g])
                 return
             for which in range(2):
@@ -269,32 +269,32 @@
 
     scale = HEAD ** -0.5
 
-    def answer(pair):
-        query_copy(pair).wait_recv()
+    def answer(pair, j):
+        if j == 0:
+            query_copy(pair).wait_recv()
         kept = row - (n - 2) * rows >= start_next
-        for j in range(PAIR):
-            head = pair * PAIR + j
-            inner[head] = against_columns(halves(asked[:, lanes(head)]), halves(inner[head]))
-
-            @pl.when(head < 2 * kv)
-            def _():
-                piece = kvbuf[n - 2, lax.div(head, kv), :, lanes(lax.rem(head, kv))]
-                inner[head] = jnp.where(kept, piece, inner[head])
+        head = pair * PAIR + j
+        inner[head] = against_columns(halves(asked[:, lanes(head)]), halves(inner[head]))
+
+        @pl.when(head < 2 * kv)
+        def _():
+            piece = kvbuf[n - 2, lax.div(head, kv), :, lanes(lax.rem(head, kv))]
+            inner[head] = jnp.where(kept, piece, inner[head])
 
     def finish_pair(pair, _):
         @pl.when((me > 0) & (me < n - 1))
         def _():
-            state_copy(pair).wait_recv()
             for j in range(PAIR):
                 head = pair * PAIR + j
+                state_copy(head).wait_recv()
                 _along, end = log_rows(head)
                 decay = jnp.exp(jnp.where(start_last < first, end, -jnp.inf))
                 inner[head] = inner[head] + decay * entered[head]
-            if pack:
-                @pl.when(me == n - 2)
-                def _():
-                    answer(pair)
-            state_copy(pair).start()
+                if pack:
+                    @pl.when(me == n - 2)
+                    def _():
+                        answer(pair, j)
+                state_copy(head).start()
 
         visible = bias[:, 0:rows] == 0.0
         carried = begin[...] < first
@@ -326,13 +326,13 @@
             sm[:, lanes(pair * PAIR + j)] = mixed[j * rows:(j + 1) * rows]
         out_copy(sm, sm_hbm, sm_sem, pair).start()
 
-        if n > 1:
-            @pl.when((me == n - 1) & (pair >= packed_pairs))
-            def _():
-                state_copy(pair).wait_recv()
-
         for j in range(PAIR):
             head = pair * PAIR + j
+            if n > 1:
+                @pl.when((me == n - 1) & (pair >= packed_pairs))
+                def _():
+                    state_copy(head).wait_recv()
+
             if pack:
                 @pl.when(me == n - 1)
                 def _():
@@ -363,7 +363,8 @@
 
         @pl.when(me < n - 1)
         def _():
-            state_copy(pair).wait_send()
+            for j in range(PAIR):
+                state_copy(pair * PAIR + j).wait_send()
 
         if pack:
             @pl.when(me == n - 1)
@@ -435,8 +436,8 @@
             pltpu.SemaphoreType.DMA((10,)),
             pltpu.SemaphoreType.DMA((n, 2)),
             pltpu.SemaphoreType.DMA((n, 2)),
-            pltpu.SemaphoreType.DMA((pairs,)),
-            pltpu.SemaphoreType.DMA((pairs,)),
+            pltpu.SemaphoreType.DMA((heads,)),
+            pltpu.SemaphoreType.DMA((heads,)),
             pltpu.SemaphoreType.DMA((pairs,)),
             pltpu.SemaphoreType.DMA((pairs,)),
             pltpu.SemaphoreType.DMA((pairs,)),

time: 46.8 us -> 45.8 us (0.979)
  Pallas kernels: 46.1 us -> 45 us
    pallas_call x1, Pallas kernels: 43.7 us -> 42.6 us  [shards(): call(doc_lengths, decay_rate, norm_gain.reshape(1, features), sm_key, sm_...]
where the time goes in v6:
time: 45.8 us; the launch traced here: 45.7 us
  Pallas kernels  45 us (98%)
  between operations  0.64 us (1%)
    pallas_call x1, Pallas kernels, shards(): call(doc_lengths, decay_rate, norm_gain.reshape(1, features), sm_key, sm_...  42.6 us
    pallas_call x1, Pallas kernels, shards(): pl.pallas_call(functools.partial(hand_over, rows), out_shape=(out, out),...  2.39 us

profile of v6, /device:TPU:24, one launch (start us, length us, event | category | flops | bytes accessed | tf_op | source)
XLA Modules:
  0.0 45.7 jit_solution(10515715894455273381)
XLA Ops:
  0.6 42.6 %shard_map.122 = (f32[128,2048]{1,0:T(8,128)}, f32[128,2048]{1,0:T(8,128)}) custom-call(s32[16]{0:T(128)} %len_ref.1, f32[16,128]{1,0:T(8,128)} %rate_hbm.1, f32[1,2048]{1,0:T(1,128)} %bitcast.1, f32[128,256]{1,0:T(8,128)} %sk_hbm.1, f32[128,256]{1,0:T(8,128)} %sv_hbm.1, f32[128,2048]{1,0:T(8,128)} %lk_hbm.1, f32[128,2048]{1,0:T(8,128)} %lv_hbm.1, ...), custom_call_target="tpu_custom_call" | custom-call | tf_op jit(solution)/shard_map/pallas_call | solution.py:450
  43.3 2.4 %shard_map.123 = (f32[128,2048]{1,0:T(8,128)}, f32[128,2048]{1,0:T(8,128)}) custom-call(f32[128,2048]{1,0:T(8,128)} %get-tuple-element.4.lin_in, f32[128,2048]{1,0:T(8,128)} %get-tuple-element.5.sm_in), custom_call_target="tpu_custom_call" | custom-call | tf_op jit(solution)/shard_map/pallas_call | solution.py:454

commit v7 on v6

--- a/solution.py
+++ b/solution.py
@@ -16,7 +16,7 @@
 HIGHEST = lax.Precision.HIGHEST
 F32 = jnp.float32
 BF16 = jnp.bfloat16
-PAIR = 2
+PAIR = 1
 PARTS = 4
 
 

time: 45.8 us -> 46.2 us (level)
  no operation moved by 1% of the time
where the time goes in v7:
time: 46.2 us; the launch traced here: 46 us
  Pallas kernels  45.4 us (98%)
  between operations  0.64 us (1%)
    pallas_call x1, Pallas kernels, shards(): call(doc_lengths, decay_rate, norm_gain.reshape(1, features), sm_key, sm_...  43 us
    pallas_call x1, Pallas kernels, shards(): pl.pallas_call(functools.partial(hand_over, rows), out_shape=(out, out),...  2.39 us

profile of v7, /device:TPU:24, one launch (start us, length us, event | category | flops | bytes accessed | tf_op | source)
XLA Modules:
  0.0 46.0 jit_solution(11111917297787074289)
XLA Ops:
  0.6 43.0 %shard_map.122 = (f32[128,2048]{1,0:T(8,128)}, f32[128,2048]{1,0:T(8,128)}) custom-call(s32[16]{0:T(128)} %len_ref.1, f32[16,128]{1,0:T(8,128)} %rate_hbm.1, f32[1,2048]{1,0:T(1,128)} %bitcast.1, f32[128,256]{1,0:T(8,128)} %sk_hbm.1, f32[128,256]{1,0:T(8,128)} %sv_hbm.1, f32[128,2048]{1,0:T(8,128)} %lk_hbm.1, f32[128,2048]{1,0:T(8,128)} %lv_hbm.1, ...), custom_call_target="tpu_custom_call" | custom-call | tf_op jit(solution)/shard_map/pallas_call | solution.py:450
  43.6 2.4 %shard_map.123 = (f32[128,2048]{1,0:T(8,128)}, f32[128,2048]{1,0:T(8,128)}) custom-call(f32[128,2048]{1,0:T(8,128)} %get-tuple-element.4.lin_in, f32[128,2048]{1,0:T(8,128)} %get-tuple-element.5.sm_in), custom_call_target="tpu_custom_call" | custom-call | tf_op jit(solution)/shard_map/pallas_call | solution.py:454
